TPU v7x, 32 devices: a whole 2x2x4 slice. The times are simulated.
32 devices in a mesh: tmpl: 4 (over y, x), row: 2 (over core), col: 4 (over z).
Axes of the slice: x: 2, y: 2, z: 4, core: 2. Of those that a mesh axis runs over, the one named last changes fastest.
Arguments:
- tmpl_act: bfloat16 [4, 4, 512, 64, 2048], P('tmpl', None, 'row', None, 'col'), may hold values from -4 to 4
- tmpl_bins: int32 [4, 4, 512, 2048], P('tmpl', None, 'row', 'col'), may hold values from 0 to 38
- tmpl_mask: int32 [4, 2048], P('tmpl'), may hold values 0 or 1
- tmpl_aatype: int32 [4, 2048], P('tmpl'), may hold values from 0 to 21
- pair_act: bfloat16 [2048, 2048, 128], P(('tmpl', 'row', 'col')), may hold values from -2.5 to 2.5
- labels: int32 [2048, 2048], P(('tmpl', 'row', 'col')), may hold values from 0 to 63
- bin_embed: bfloat16 [39, 64], replicated, may hold values from -4 to 4
- row_embed: bfloat16 [22, 64], replicated, may hold values from -4 to 4
- col_embed: bfloat16 [22, 64], replicated, may hold values from -4 to 4
- mask_embed: float32 [64], replicated, may hold values from -4 to 4
- layer_gain: float32 [2, 64], replicated, may hold values from 0.1 to 1.9
- w_in: bfloat16 [2, 64, 128], replicated, may hold values from -0.75 to 0.75
- w_out: bfloat16 [2, 128, 64], replicated, may hold values from -0.5 to 0.5
- final_gain: float32 [64], replicated, may hold values from 0.1 to 1.9
- w_query: bfloat16 [128, 64], replicated, may hold values from -0.5 to 0.5
- w_keyval: bfloat16 [64, 128], replicated, may hold values from -0.75 to 0.75
- w_output: bfloat16 [64, 128], replicated, may hold values from -0.75 to 0.75
- head_weight: bfloat16 [128, 64], replicated, may hold values from -0.44921875 to 0.44921875
- head_bias: float32 [64], replicated, may hold values from -3 to 3
Outputs:
- mean_loss: float32 [], replicated
- head_grad: float32 [128, 64], replicated
- bias_grad: float32 [64], replicated
- output_grad: float32 [64, 128], replicated
All inputs are finite; a program needn't handle non-finite values. No bound on the sum of `tmpl_mask` on one device may be relied on, other than what follows from the above.
Results may differ from a plain program's by a relative error of at most 0.0003.
Values may be sent and summed in bfloat16 or wider, within the bound.
A program may use at most 512 MiB of HBM per device.

v0:
```python
import math

import jax
import jax.numpy as jnp
from jax import lax
from jax.sharding import PartitionSpec as P

HEADS = 4
HEAD_DIM = 16


CLIP_NORM = 16.0


def layer_norm(inputs, gain_vector, channel_axis):
    average = jnp.mean(inputs, axis=channel_axis, keepdims=True)
    centered = inputs - average
    spread = jnp.mean(centered * centered, axis=channel_axis, keepdims=True)
    return centered * lax.rsqrt(spread + 1e-05) * gain_vector


def on_device(
    tmpl_act,
    tmpl_bins,
    tmpl_mask,
    tmpl_aatype,
    pair_act,
    labels,
    bin_embed,
    row_embed,
    col_embed,
    mask_embed,
    layer_gain,
    w_in,
    w_out,
    final_gain,
    w_query,
    w_keyval,
    w_output,
    head_weight,
    head_bias,
):
    group_count = lax.axis_size("tmpl")
    col_count = lax.axis_size("col")
    residues = tmpl_mask.shape[1]
    group_rows = tmpl_bins.shape[2]
    col_width = tmpl_bins.shape[3]
    row_count = group_rows // col_count
    channels = tmpl_act.shape[3]
    pair_width = pair_act.shape[2]
    head_width = w_query.shape[1]
    row_offset = lax.axis_index("row") * group_rows
    col_offset = lax.axis_index("col") * col_width
    mask_table = tmpl_mask[0].astype(jnp.float32)
    type_table = tmpl_aatype[0]
    kinds = jnp.arange(row_embed.shape[0], dtype=jnp.int32)
    levels = jnp.arange(bin_embed.shape[0], dtype=jnp.int32)
    col_mask = lax.dynamic_slice_in_dim(mask_table, col_offset, col_width)
    col_types = lax.dynamic_slice_in_dim(type_table, col_offset, col_width)
    col_onehot = (col_types[None, :] == kinds[:, None]).astype(jnp.bfloat16)
    col_term = jnp.einsum("aj,ac->cj", col_onehot, col_embed, preferred_element_type=jnp.float32)

    def embed_group(group_item):
        previous, bin_codes, group_index = group_item
        offset = group_index * (residues // group_count) + row_offset
        row_mask = lax.dynamic_slice_in_dim(mask_table, offset, group_rows).reshape(
            col_count, row_count
        )
        row_types = lax.dynamic_slice_in_dim(type_table, offset, group_rows).reshape(
            col_count, row_count
        )
        row_onehot = (row_types[None] == kinds[:, None, None]).astype(jnp.bfloat16)
        row_term = jnp.einsum(
            "anr,ac->nrc", row_onehot, row_embed, preferred_element_type=jnp.float32
        )
        bin_codes = bin_codes.reshape(col_count, row_count, col_width)
        bin_onehot = (bin_codes[None] == levels[:, None, None, None]).astype(jnp.bfloat16)
        bin_term = jnp.einsum(
            "bnrj,bc->nrcj", bin_onehot, bin_embed, preferred_element_type=jnp.float32
        )
        pair_mask = row_mask[:, :, None] * col_mask[None, None, :]
        tmpl_state = previous.reshape(col_count, row_count, channels, col_width).astype(jnp.float32)
        tmpl_state = (
            tmpl_state
            + pair_mask[:, :, None, :] * (bin_term + mask_embed[:, None])
            + row_term[:, :, :, None]
            + col_term[None, None]
        )
        for layer_index in range(w_in.shape[0]):
            normed = layer_norm(tmpl_state, layer_gain[layer_index][:, None], 2).astype(
                jnp.bfloat16
            )
            hidden = jax.nn.relu(
                jnp.einsum(
                    "nrcj,ce->nrej", normed, w_in[layer_index], preferred_element_type=jnp.float32
                )
            ).astype(jnp.bfloat16)
            tmpl_state = tmpl_state + jnp.einsum(
                "nrej,ec->nrcj", hidden, w_out[layer_index], preferred_element_type=jnp.float32
            )
        return layer_norm(tmpl_state, final_gain[:, None], 2).astype(jnp.bfloat16)

    features = lax.map(
        embed_group, (tmpl_act[0], tmpl_bins[0], jnp.arange(group_count, dtype=jnp.int32))
    )
    moved = lax.all_to_all(
        features.reshape(1, group_count * col_count, row_count, channels, col_width),
        ("tmpl", "col"),
        split_axis=1,
        concat_axis=0,
        tiled=True,
    )
    moved = moved.reshape(group_count, col_count, row_count, channels, col_width)
    pair_rows = pair_act.reshape(row_count, col_count, col_width, pair_width)
    queries = jnp.einsum(
        "rnjz,zk->nrkj", pair_rows, w_query, preferred_element_type=jnp.float32
    ).astype(jnp.bfloat16)
    queries = queries.reshape(col_count, row_count, HEADS, HEAD_DIM, col_width)
    keyval = jnp.einsum(
        "snrcj,ck->snrkj", moved, w_keyval, preferred_element_type=jnp.float32
    ).astype(jnp.bfloat16)
    key_heads = keyval[:, :, :, :head_width].reshape(
        group_count, col_count, row_count, HEADS, HEAD_DIM, col_width
    )
    value_heads = keyval[:, :, :, head_width:].reshape(
        group_count, col_count, row_count, HEADS, HEAD_DIM, col_width
    )
    scores = jnp.einsum(
        "nrhdj,snrhdj->snrhj", queries, key_heads, preferred_element_type=jnp.float32
    ) / math.sqrt(HEAD_DIM)
    exp_scores = jnp.exp(scores)
    weights = (exp_scores / jnp.sum(exp_scores, axis=0, keepdims=True)).astype(jnp.bfloat16)
    mixture = jnp.einsum(
        "snrhj,snrhdj->nrhdj", weights, value_heads, preferred_element_type=jnp.float32
    ).astype(jnp.bfloat16)
    mixture = mixture.reshape(col_count, row_count, head_width, col_width)
    update = jnp.einsum("nrkj,kz->rnjz", mixture, w_output, preferred_element_type=jnp.float32)
    new_pair = (pair_rows.astype(jnp.float32) + update).astype(jnp.bfloat16)
    logits = (
        jnp.einsum("rnjz,zb->rnjb", new_pair, head_weight, preferred_element_type=jnp.float32)
        + head_bias
    )
    exp_logits = jnp.exp(logits)
    partition = jnp.sum(exp_logits, axis=-1, keepdims=True)
    classes = jnp.arange(head_weight.shape[1], dtype=jnp.int32)
    target = (labels.reshape(row_count, col_count, col_width)[..., None] == classes).astype(
        jnp.float32
    )
    cross_entropy = jnp.log(partition[..., 0]) - jnp.sum(target * logits, axis=-1)
    loss_part = jnp.sum(cross_entropy)
    logit_grad = ((exp_logits / partition - target) / residues).astype(jnp.bfloat16)
    head_part = jnp.einsum(
        "rnjz,rnjb->zb", new_pair, logit_grad, preferred_element_type=jnp.float32
    )
    bias_part = jnp.sum(logit_grad.astype(jnp.float32), axis=(0, 1, 2))
    pair_grad = jnp.einsum(
        "rnjb,zb->rnjz", logit_grad, head_weight, preferred_element_type=jnp.float32
    ).astype(jnp.bfloat16)
    output_part = jnp.einsum(
        "nrkj,rnjz->kz", mixture, pair_grad, preferred_element_type=jnp.float32
    )
    loss_sum, head_sum, bias_sum, output_sum = lax.psum(
        (loss_part, head_part, bias_part, output_part), ("tmpl", "row", "col")
    )
    squares = (
        jnp.sum(head_sum * head_sum)
        + jnp.sum(bias_sum * bias_sum)
        + jnp.sum(output_sum * output_sum)
    )
    factor = CLIP_NORM / jnp.maximum(jnp.sqrt(squares), CLIP_NORM)
    head_grad = head_sum * factor
    output_grad = output_sum * factor
    return (loss_sum / float(residues * residues), head_grad, bias_sum * factor, output_grad)


def solution(mesh):
    in_specs = (
        P("tmpl", None, "row", None, "col"),
        P("tmpl", None, "row", "col"),
        P("tmpl", None),
        P("tmpl", None),
        P(("tmpl", "row", "col"), None, None),
        P(("tmpl", "row", "col"), None),
        P(),
        P(),
        P(),
        P(),
        P(),
        P(),
        P(),
        P(),
        P(),
        P(),
        P(),
        P(),
        P(),
    )
    out_specs = (P(), P(), P(), P())
    return jax.shard_map(
        on_device, mesh=mesh, in_specs=in_specs, out_specs=out_specs, check_vma=False
    )
```

profile of v0, /device:TPU:10, one launch (start us, length us, event | category | flops | bytes accessed | tf_op | source)
XLA Modules:
  0.0 2648.2 jit_solution(2894960302181089265)
XLA Ops:
  3.0 680.3 %while.11 = (s32[]{:T(128)}, bf16[4,4,64,64,512]{4,3,2,1,0:T(8,128)(2,1)}, bf16[4,256,64,512]{3,2,1,0:T(8,128)(2,1)}, s32[4]{0:T(128)S(1)}, s32[]{:T(128)}, /*in...) while((s32[]{:T(128)}, ...), condition=%wide.region_7.8_spmd.clone, body=%wide.region_0.7_spmd.clone.sunk | while | flops 9586153472 | bytes 587840128 | solution.py:103
  15.5 17.4 fusion.97
  46.8 41.1 %fusion.98 = (f32[4,64,512]{2,1,0:T(8,128)S(1)}, f32[4,64,64,512]{3,2,1,0:T(8,128)}) fusion(f32[4,64,64,512]{3,2,1,0:T(8,128)} %get-tuple-element.303, bf16[2,128,64]{1,2,0:T(8,128)(2,1)S(1)} %copy-done.4, f32[64]{0:T(128)S(1)} %get-tuple-element.304, f32[4,64,512]{2,1,0:T(8,128)S(1)} %add_rsqrt_fusion.6, ...), kind=kOutput, calls=%fused_computation.101.clone.1 | convolution fusion | flops 4378722304 | bytes 102269440 | tf_op jit(solution)/shard_map/while/body/eval_jaxpr/nrej,ec->nrcj/dot_general | solution.py:98
  101.7 41.1 %fusion.99 = (f32[4,64,512]{2,1,0:T(8,128)S(1)}, f32[4,64,64,512]{3,2,1,0:T(8,128)}) fusion(f32[4,64,64,512]{3,2,1,0:T(8,128)} %get-tuple-element.306, bf16[2,128,64]{1,2,0:T(8,128)(2,1)S(1)} %copy-done.4, f32[64]{0:T(128)S(1)} %get-tuple-element.307, f32[4,64,512]{2,1,0:T(8,128)S(1)} %add_rsqrt_fusion.7, ...), kind=kOutput, calls=%fused_computation.102.clone.1 | convolution fusion | flops 4378722304 | bytes 102269440 | tf_op jit(solution)/shard_map/while/body/eval_jaxpr/nrej,ec->nrcj/dot_general | solution.py:98
  185.5 17.4 fusion.97
  216.8 41.1 %fusion.98 = (f32[4,64,512]{2,1,0:T(8,128)S(1)}, f32[4,64,64,512]{3,2,1,0:T(8,128)}) fusion(f32[4,64,64,512]{3,2,1,0:T(8,128)} %get-tuple-element.303, bf16[2,128,64]{1,2,0:T(8,128)(2,1)S(1)} %copy-done.4, f32[64]{0:T(128)S(1)} %get-tuple-element.304, f32[4,64,512]{2,1,0:T(8,128)S(1)} %add_rsqrt_fusion.6, ...), kind=kOutput, calls=%fused_computation.101.clone.1 | convolution fusion | flops 4378722304 | bytes 102269440 | tf_op jit(solution)/shard_map/while/body/eval_jaxpr/nrej,ec->nrcj/dot_general | solution.py:98
  271.7 41.1 %fusion.99 = (f32[4,64,512]{2,1,0:T(8,128)S(1)}, f32[4,64,64,512]{3,2,1,0:T(8,128)}) fusion(f32[4,64,64,512]{3,2,1,0:T(8,128)} %get-tuple-element.306, bf16[2,128,64]{1,2,0:T(8,128)(2,1)S(1)} %copy-done.4, f32[64]{0:T(128)S(1)} %get-tuple-element.307, f32[4,64,512]{2,1,0:T(8,128)S(1)} %add_rsqrt_fusion.7, ...), kind=kOutput, calls=%fused_computation.102.clone.1 | convolution fusion | flops 4378722304 | bytes 102269440 | tf_op jit(solution)/shard_map/while/body/eval_jaxpr/nrej,ec->nrcj/dot_general | solution.py:98
  355.6 17.4 fusion.97
  386.9 41.1 %fusion.98 = (f32[4,64,512]{2,1,0:T(8,128)S(1)}, f32[4,64,64,512]{3,2,1,0:T(8,128)}) fusion(f32[4,64,64,512]{3,2,1,0:T(8,128)} %get-tuple-element.303, bf16[2,128,64]{1,2,0:T(8,128)(2,1)S(1)} %copy-done.4, f32[64]{0:T(128)S(1)} %get-tuple-element.304, f32[4,64,512]{2,1,0:T(8,128)S(1)} %add_rsqrt_fusion.6, ...), kind=kOutput, calls=%fused_computation.101.clone.1 | convolution fusion | flops 4378722304 | bytes 102269440 | tf_op jit(solution)/shard_map/while/body/eval_jaxpr/nrej,ec->nrcj/dot_general | solution.py:98
  441.8 41.1 %fusion.99 = (f32[4,64,512]{2,1,0:T(8,128)S(1)}, f32[4,64,64,512]{3,2,1,0:T(8,128)}) fusion(f32[4,64,64,512]{3,2,1,0:T(8,128)} %get-tuple-element.306, bf16[2,128,64]{1,2,0:T(8,128)(2,1)S(1)} %copy-done.4, f32[64]{0:T(128)S(1)} %get-tuple-element.307, f32[4,64,512]{2,1,0:T(8,128)S(1)} %add_rsqrt_fusion.7, ...), kind=kOutput, calls=%fused_computation.102.clone.1 | convolution fusion | flops 4378722304 | bytes 102269440 | tf_op jit(solution)/shard_map/while/body/eval_jaxpr/nrej,ec->nrcj/dot_general | solution.py:98
  556.8 41.1 %fusion.98 = (f32[4,64,512]{2,1,0:T(8,128)S(1)}, f32[4,64,64,512]{3,2,1,0:T(8,128)}) fusion(f32[4,64,64,512]{3,2,1,0:T(8,128)} %get-tuple-element.303, bf16[2,128,64]{1,2,0:T(8,128)(2,1)S(1)} %copy-done.4, f32[64]{0:T(128)S(1)} %get-tuple-element.304, f32[4,64,512]{2,1,0:T(8,128)S(1)} %add_rsqrt_fusion.6, ...), kind=kOutput, calls=%fused_computation.101.clone.1 | convolution fusion | flops 4378722304 | bytes 102269440 | tf_op jit(solution)/shard_map/while/body/eval_jaxpr/nrej,ec->nrcj/dot_general | solution.py:98
  611.7 41.1 %fusion.99 = (f32[4,64,512]{2,1,0:T(8,128)S(1)}, f32[4,64,64,512]{3,2,1,0:T(8,128)}) fusion(f32[4,64,64,512]{3,2,1,0:T(8,128)} %get-tuple-element.306, bf16[2,128,64]{1,2,0:T(8,128)(2,1)S(1)} %copy-done.4, f32[64]{0:T(128)S(1)} %get-tuple-element.307, f32[4,64,512]{2,1,0:T(8,128)S(1)} %add_rsqrt_fusion.7, ...), kind=kOutput, calls=%fused_computation.102.clone.1 | convolution fusion | flops 4378722304 | bytes 102269440 | tf_op jit(solution)/shard_map/while/body/eval_jaxpr/nrej,ec->nrcj/dot_general | solution.py:98
  691.8 21.0 convolution_convert_fusion
  712.8 1487.5 %all-to-all-done = bf16[1,16,64,64,512]{4,3,2,0,1:T(8,128)(2,1)} async-done(((bf16[1,16,64,64,512]{4,3,2,0,1:T(8,128)(2,1)}), bf16[1,16,64,64,512]{4,3,2,0,1:T(8,128)(2,1)}, u32[]{:S(2)}, u32[]{:S(2)}) %all-to-all-start) | async-done | bytes 67108896 | tf_op jit(solution)/shard_map/all_to_all | solution.py:106
  2200.3 70.4 %convert_bitcast_fusion = bf16[4,4,64,128,512]{4,3,2,1,0:T(8,128)(2,1)} fusion(bf16[4,4,64,64,512]{4,3,2,1,0:T(8,128)(2,1)} %bitcast.13, bf16[64,128]{1,0:T(8,128)(2,1)S(1)} %copy-done), kind=kOutput, calls=%fused_computation.58 | convolution fusion | flops 8657043456 | bytes 201342976 | tf_op jit(solution)/shard_map/snrcj,ck->snrkj/dot_general | solution.py:119
  2270.7 86.5 %fusion.77 = (bf16[4,4,64,64,512]{4,3,2,1,0:T(8,128)(2,1)}, bf16[4,4,64,64,512]{4,3,2,1,0:T(8,128)(2,1)}) fusion(bf16[4,4,64,128,512]{4,3,2,1,0:T(8,128)(2,1)} %convert_bitcast_fusion), kind=kLoop, calls=%fused_computation.103 | loop fusion | bytes 268435456 | tf_op jit(solution)/shard_map/slice | solution.py:122
  2357.2 49.6 %multiply_reduce_fusion.4 = f32[4,64,4,512,4]{3,2,1,0,4:T(4,128)S(1)} fusion(bf16[4,4,64,64,512]{4,3,2,1,0:T(8,128)(2,1)} %get-tuple-element.189, bf16[4,64,4,512,16]{3,4,2,0,1:T(8,128)(2,1)} %bitcast.191), kind=kLoop, calls=%fused_computation.57 | loop fusion | flops 98566144 | bytes 92274688
  2427.6 49.1 %multiply_reduce_fusion.3 = bf16[4,64,4,512,16]{3,4,2,1,0:T(8,128)(2,1)} fusion(bf16[4,64,4,512,4,16]{3,5,2,1,0,4:T(8,128)(2,1)} %bitcast.2, f32[4,64,4,512,4]{3,2,1,0,4:T(4,128)} %copy.72), kind=kLoop, calls=%fused_computation.56 | loop fusion | flops 92274688 | bytes 92274688 | tf_op jit(solution)/shard_map/snrhj,snrhdj->nrhdj/dot_general | solution.py:133
  2476.7 27.6 %fusion.42 = bf16[64,4,512,128]{3,2,0,1:T(8,128)(2,1)} fusion(bf16[4,64,64,512]{3,2,1,0:T(8,128)(2,1)} %bitcast.189, bf16[64,4,512,128]{3,2,1,0:T(8,128)(2,1)} %bitcast.188, bf16[64,128]{1,0:T(8,128)(2,1)S(1)} %copy-done.8), kind=kOutput, calls=%fused_computation.60 | convolution fusion | flops 2197815296 | bytes 83902464 | tf_op jit(solution)/shard_map/nrkj,kz->rnjz/dot_general | solution.py:137
  2504.3 26.7 %exponential_reduce_fusion = (f32[64,4,512]{2,1,0:T(4,128)S(1)}, f32[64,4,512]{2,1,0:T(4,128)S(1)}, f32[64,4,512,64]{2,3,1,0:T(8,128)}) fusion(f32[64]{0:T(128)S(1)} %copy-done.10, s32[64,4,512]{2,1,0:T(4,128)S(1)} %copy-done.3, bf16[128,64]{0,1:T(8,128)(2,1)S(1)} %copy-done.11, bf16[64,4,512,128]{3,2,0,1:T(8,128)(2,1)} %fusion.42), kind=kOutput, calls=%fused_computation.69 | convolution fusion | flops 2189164544 | bytes 68698368 | tf_op jit(solution)/shard_map/rnjz,zb->rnjb/dot_general | solution.py:140
  2531.0 22.2 convert_reduce_fusion
  2553.2 22.7 fusion.58
  2575.9 19.2 fusion.55
  2596.0 44.4 %all-reduce.2 = (f32[]{:T(128)}, f32[128,64]{0,1:T(8,128)S(1)}, f32[64]{0:T(128)S(1)}, f32[64,128]{1,0:T(8,128)S(1)}) all-reduce(f32[]{:T(128)} %subtract_reduce_fusion, f32[128,64]{0,1:T(8,128)S(1)} %fusion.55, f32[64]{0:T(128)S(1)} %get-tuple-element.179, ...), channel_id=1, replica_groups=mesh['tmpl'=4,'row'=2,'col'=4] {'tmpl','row','col'}, use_global_device_ids=true, to_apply=%region_12.13 | all-reduce | flops 16449 | bytes 131592 | tf_op jit(solution)/shard_map/psum | solution.py:162
  (169 shorter events, 331.8 us)
Async XLA Ops:
  0.6 2199.7 %copy-start = (bf16[64,128]{1,0:T(8,128)(2,1)S(1)}, bf16[64,128]{1,0:T(8,128)(2,1)}, u32[]{:S(2)}) copy-start(bf16[64,128]{1,0:T(8,128)(2,1)} %param.36) | copy-start | bytes 49156
  32.9 13.8 copy-start.6
  32.9 13.8 copy-start.2
  32.9 13.8 copy-start.4
  142.8 20.2 copy-start.1
  142.8 20.2 copy-start.9
  203.0 13.8 copy-start.6
  203.0 13.8 copy-start.2
  203.0 13.8 copy-start.4
  312.8 20.2 copy-start.1
  312.8 20.2 copy-start.9
  373.0 13.8 copy-start.2
  373.0 13.8 copy-start.4
  482.9 20.2 copy-start.1
  482.9 20.2 copy-start.9
  543.0 13.8 copy-start.2
  543.0 13.8 copy-start.4
  652.8 20.2 copy-start.1
  652.8 20.2 copy-start.9
  683.3 1517.0 %all-to-all-start = ((bf16[1,16,64,64,512]{4,3,2,0,1:T(8,128)(2,1)}), bf16[1,16,64,64,512]{4,3,2,0,1:T(8,128)(2,1)}, u32[]{:S(2)}, u32[]{:S(2)}) async-start(bf16[1,16,64,64,512]{4,3,2,0,1:T(8,128)(2,1)} %bitcast.12), calls=%async_computation | async-start | bytes 134217728 | tf_op jit(solution)/shard_map/all_to_all | solution.py:106
  2427.6 49.1 %copy-start.8 = (bf16[64,128]{1,0:T(8,128)(2,1)S(1)}, bf16[64,128]{1,0:T(8,128)(2,1)}, u32[]{:S(2)}) copy-start(bf16[64,128]{1,0:T(8,128)(2,1)} %param.37) | copy-start | bytes 49156
  2476.7 27.6 %copy-start.3 = (s32[64,4,512]{2,1,0:T(4,128)S(1)}, s32[64,4,512]{2,1,0:T(4,128)}, u32[]{:S(2)}) copy-start(s32[64,4,512]{2,1,0:T(4,128)} %eq.64) | copy-start | bytes 1572868
  2476.7 27.6 %copy-start.10 = (f32[64]{0:T(128)S(1)}, f32[64]{0:T(128)}, u32[]{:S(2)}) copy-start(f32[64]{0:T(128)} %param.39) | copy-start | bytes 772
  2476.7 27.6 %copy-start.11 = (bf16[128,64]{0,1:T(8,128)(2,1)S(1)}, bf16[128,64]{0,1:T(8,128)(2,1)}, u32[]{:S(2)}) copy-start(bf16[128,64]{0,1:T(8,128)(2,1)} %param.38) | copy-start | bytes 49156
  (12 other events, 143.4 us)
where the time goes:
time: 2660 us; the launch traced here: 2650 us
  waiting for transfers between devices  1490 us (56%)
  matrix products  591 us (22%)
  other arithmetic  352 us (13%)
  local copies, waits for them, and re-layouts  158 us (6%)
  blocking collectives  44.4 us (2%)
    all_to_all x1, waiting for transfers between devices, on_device(): lax.all_to_all(features.reshape(1, group_count * col_count, row_count, ch...  1490 us
    dot_general x8, matrix products, embed_group(): jnp.einsum('nrej,ec->nrcj', hidden, w_out[layer_index], preferred_element...  329 us
    reduce_sum x12, other arithmetic, layer_norm(): spread = jnp.mean(centered * centered, axis=channel_axis, keepdims=True)  175 us
    slice x1, local copies, waits for them, and re-layouts, on_device(): keyval[:, :, :, :head_width]  86.5 us
    dot_general x1, matrix products, on_device(): jnp.einsum('snrcj,ck->snrkj', moved, w_keyval, preferred_element_type=jnp...  70.4 us
    dot_general x4, matrix products, embed_group(): jnp.einsum('bnrj,bc->nrcj', bin_onehot, bin_embed, preferred_element_type...  69.8 us
    unnamed x2, other arithmetic  54.6 us
  transfers between devices with their start and end apart: 1, of which 1 were waited for; matrix products, arithmetic and copies ran while one was open for 1% of the time, Pallas kernels for 0%

commit v1 on v0

v1 whole, which is shorter than its diff:
```python
import functools
import math

import jax
import jax.numpy as jnp
from jax import lax
from jax.experimental import pallas as pl
from jax.experimental.pallas import tpu as pltpu
from jax.sharding import PartitionSpec as P

HEADS = 4
HEAD_DIM = 16
CLIP_NORM = 16.0
TILE = 16
BF16 = jnp.bfloat16
F32 = jnp.float32


def padded(size):
    return -(-size // TILE) * TILE


def pad_columns(matrix):
    return jnp.pad(matrix, ((0, 0), (0, padded(matrix.shape[1]) - matrix.shape[1])))


def layer_norm(state, gain):
    count = state.shape[0]
    average = jnp.sum(state, axis=0, keepdims=True) * (1.0 / count)
    centered = state - average
    spread = jnp.sum(centered * centered, axis=0, keepdims=True) * (1.0 / count)
    return (centered * lax.rsqrt(spread + 1e-05) * gain).astype(BF16)


def dot(left, right):
    return lax.dot_general(left, right, (((1,), (0,)), ((), ())), preferred_element_type=F32)


def dot_lanes(left, right):
    return lax.dot_general(left, right, (((1,), (1,)), ((), ())), preferred_element_type=F32)


def template_kernel(
    levels,
    together,
    place_ref,
    mask_ref,
    type_ref,
    act_ref,
    bins_ref,
    colmask_ref,
    colhot_ref,
    embed_ref,
    gains_ref,
    w_in_ref,
    w_out_ref,
    out_ref,
):
    rows = act_ref.shape[1]
    width = act_ref.shape[3]
    offset = place_ref[2] + pl.program_id(0) * rows
    level_rows = padded(levels + 3)
    kind_rows = colhot_ref.shape[0]
    layers = w_in_ref.shape[0]

    def some_rows(step, carry):
        level_iota = lax.broadcasted_iota(jnp.int32, (level_rows, width), 0)
        least = jnp.where(
            level_iota < levels, level_iota, jnp.where(level_iota < levels + 3, 0, levels)
        )
        most = jnp.where(
            level_iota < levels, level_iota, jnp.where(level_iota < levels + 3, levels - 1, -1)
        )
        kind_iota = lax.broadcasted_iota(jnp.int32, (kind_rows, width), 0)
        states = []
        for inner in range(together):
            row = step * together + inner
            row_mask = mask_ref[offset + row]
            row_type = type_ref[offset + row]
            codes = bins_ref[0, pl.ds(row, 1), :]
            codes = jnp.where(colmask_ref[...] * row_mask > 0, codes, -1)
            hot = jnp.where((codes >= least) & (codes <= most), 1.0, 0.0).astype(BF16)
            row_hot = jnp.where(kind_iota == row_type, 1.0, 0.0).astype(BF16)
            parts = jnp.concatenate([act_ref[0, row], hot, colhot_ref[...], row_hot], axis=0)
            states.append(dot(embed_ref[...], parts))
        for layer in range(layers):
            normed = [layer_norm(state, gains_ref[layer]) for state in states]
            hidden = [jnp.maximum(dot(w_in_ref[layer], one).astype(BF16), 0) for one in normed]
            states = [state + dot(w_out_ref[layer], one) for state, one in zip(states, hidden)]
        for inner in range(together):
            out_ref[step * together + inner] = layer_norm(states[inner], gains_ref[layers])
        return carry

    lax.fori_loop(0, rows // together, some_rows, 0)


def template_features(
    act, bins, place, masks, types, colmask, colhot, embed, gains, w_in, w_out, levels, row_count
):
    channels, width = act.shape[2:]
    block = math.gcd(8, row_count)
    together = math.gcd(4, block)
    whole = lambda array: pl.BlockSpec(array.shape, lambda r, *_: (0,) * array.ndim)
    pairs = row_count * width
    grid_spec = pltpu.PrefetchScalarGridSpec(
        num_scalar_prefetch=3,
        grid=(row_count // block,),
        in_specs=[
            pl.BlockSpec(
                (1, block, channels, width),
                lambda r, place, *_: (place[0], place[1] * (row_count // block) + r, 0, 0),
            ),
            pl.BlockSpec(
                (1, block, width),
                lambda r, place, *_: (place[0], place[1] * (row_count // block) + r, 0),
            ),
            whole(colmask),
            whole(colhot),
            whole(embed),
            whole(gains),
            whole(w_in),
            whole(w_out),
        ],
        out_specs=pl.BlockSpec((block, channels, width), lambda r, *_: (r, 0, 0)),
    )
    return pl.pallas_call(
        functools.partial(template_kernel, levels, together),
        grid_spec=grid_spec,
        out_shape=jax.ShapeDtypeStruct((row_count, channels, width), BF16),
        compiler_params=pltpu.CompilerParams(vmem_limit_bytes=48 * 2**20),
        cost_estimate=pl.CostEstimate(
            flops=pairs * 2 * 256 * 448, bytes_accessed=pairs * channels * 4, transcendentals=0
        ),
        name="template_features",
    )(place, masks, types, act, bins, colmask, colhot, embed, gains, w_in, w_out)


def pair_kernel(
    together,
    residues,
    *refs,
):
    feature_refs = refs[:-11]
    (
        pair_ref,
        labels_ref,
        w_first_ref,
        w_keyval_ref,
        w_output_ref,
        head_t_ref,
        head_ref,
        bias_ref,
        loss_ref,
        head_part_ref,
        output_part_ref,
    ) = refs[-11:]
    rows, width, pair_width = pair_ref.shape
    bins = head_ref.shape[1]
    head_width = HEADS * HEAD_DIM

    @pl.when(pl.program_id(0) == 0)
    def _():
        loss_ref[...] = jnp.zeros_like(loss_ref)
        head_part_ref[...] = jnp.zeros_like(head_part_ref)
        output_part_ref[...] = jnp.zeros_like(output_part_ref)

    def some_rows(step, carry):
        class_iota = lax.broadcasted_iota(jnp.int32, (bins, width), 0)
        ones = jnp.ones((TILE, width), BF16)
        kept = []
        for inner in range(together):
            row = step * together + inner
            first = dot_lanes(w_first_ref[...], pair_ref[row])
            queries = first[:head_width].astype(BF16).astype(F32)
            scores, values = [], []
            for feature_ref in feature_refs:
                keyval = dot(w_keyval_ref[...], feature_ref[row]).astype(BF16).astype(F32)
                product = (queries * keyval[:head_width]).reshape(HEADS, HEAD_DIM, width)
                scores.append(
                    jnp.exp(jnp.sum(product, axis=1, keepdims=True) * (1.0 / math.sqrt(HEAD_DIM)))
                )
                values.append(keyval[head_width:].reshape(HEADS, HEAD_DIM, width))
            inverse = 1.0 / functools.reduce(jnp.add, scores)
            mixture = functools.reduce(
                jnp.add,
                [
                    (score * inverse).astype(BF16).astype(F32) * value
                    for score, value in zip(scores, values)
                ],
            )
            mixture = mixture.reshape(head_width, width).astype(BF16)
            kept.append((row, first[head_width:], mixture))
        for row, pair, mixture in kept:
            new_pair = (pair + dot(w_output_ref[...], mixture)).astype(BF16)
            logits = dot(head_t_ref[...], new_pair) + bias_ref[...]
            exp_logits = jnp.exp(logits)
            partition = jnp.sum(exp_logits, axis=0, keepdims=True)
            target = class_iota == labels_ref[pl.ds(row, 1), :]
            picked = jnp.sum(jnp.where(target, logits, 0.0), axis=0, keepdims=True)
            loss_ref[...] += jnp.log(partition) - picked
            softmax = exp_logits * (1.0 / partition)
            grad = (jnp.where(target, softmax - 1.0, softmax) * (1.0 / residues)).astype(BF16)
            head_part_ref[...] += dot_lanes(grad, jnp.concatenate([new_pair, ones], axis=0))
            pair_grad = dot(head_ref[...], grad).astype(BF16)
            output_part_ref[...] += dot_lanes(mixture, pair_grad)
        return carry

    lax.fori_loop(0, rows // together, some_rows, 0)


def pair_sums(features, pair, labels, weights, residues):
    row_count, width, pair_width = pair.shape
    channels = features[0].shape[1]
    block = math.gcd(8, row_count)
    together = math.gcd(2, block)
    bins = weights[4].shape[1]
    whole = lambda array: pl.BlockSpec(array.shape, lambda r: (0,) * array.ndim)
    blocked = lambda array: pl.BlockSpec(
        (block,) + array.shape[1:], lambda r: (r,) + (0,) * (array.ndim - 1)
    )
    shapes = [
        (1, width),
        (bins, pair_width + TILE),
        (HEADS * HEAD_DIM, pair_width),
    ]
    pairs = row_count * width
    return pl.pallas_call(
        functools.partial(pair_kernel, together, residues),
        grid=(row_count // block,),
        in_specs=[blocked(one) for one in features]
        + [blocked(pair), blocked(labels)]
        + [whole(one) for one in weights],
        out_specs=[pl.BlockSpec(shape, lambda r: (0, 0)) for shape in shapes],
        out_shape=[jax.ShapeDtypeStruct(shape, F32) for shape in shapes],
        compiler_params=pltpu.CompilerParams(vmem_limit_bytes=48 * 2**20),
        cost_estimate=pl.CostEstimate(
            flops=pairs * 2 * 256 * 1152,
            bytes_accessed=pairs * (len(features) * channels + pair_width) * 2,
            transcendentals=0,
        ),
        name="pair_sums",
    )(*features, pair, labels, *weights)


def partners(count, step):
    if count & (count - 1) == 0:
        return [(one, one ^ step) for one in range(count)]
    return [(one, (one + step) % count) for one in range(count)]


def towards(me, count, step):
    if count & (count - 1) == 0:
        return me ^ step
    return lax.rem(me + step, count)


def origin(me, count, step):
    if count & (count - 1) == 0:
        return me ^ step
    return lax.rem(me - step + count, count)


def on_device(
    tmpl_act,
    tmpl_bins,
    tmpl_mask,
    tmpl_aatype,
    pair_act,
    labels,
    bin_embed,
    row_embed,
    col_embed,
    mask_embed,
    layer_gain,
    w_in,
    w_out,
    final_gain,
    w_query,
    w_keyval,
    w_output,
    head_weight,
    head_bias,
):
    group_count = lax.axis_size("tmpl")
    col_count = lax.axis_size("col")
    residues = tmpl_mask.shape[1]
    group_rows = tmpl_bins.shape[2]
    col_width = tmpl_bins.shape[3]
    row_count = group_rows // col_count
    channels = tmpl_act.shape[3]
    pair_width = pair_act.shape[2]
    tmpl_me = lax.axis_index("tmpl")
    col_me = lax.axis_index("col")
    row_offset = lax.axis_index("row") * group_rows
    levels = bin_embed.shape[0]
    kinds = row_embed.shape[0]

    def pair_block(array, block):
        return lax.dynamic_slice_in_dim(array, block * col_width, col_width, axis=1)

    pair_parts, label_parts = [], []
    for step in range(col_count):
        block = towards(col_me, col_count, step)
        pair, label = pair_block(pair_act, block), pair_block(labels, block)
        if step:
            pair = lax.ppermute(pair, "col", partners(col_count, step))
            label = lax.ppermute(label, "col", partners(col_count, step))
        pair_parts.append(pair)
        label_parts.append(label)

    masks, types = tmpl_mask[0], tmpl_aatype[0]
    col_offset = col_me * col_width
    colmask = lax.dynamic_slice_in_dim(masks, col_offset, col_width)[None, :]
    col_types = lax.dynamic_slice_in_dim(types, col_offset, col_width)
    kind_iota = jnp.arange(padded(kinds), dtype=jnp.int32)
    colhot = (col_types[None, :] == kind_iota[:, None]).astype(BF16)
    high = lax.reduce_precision(mask_embed, 8, 7)
    middle = lax.reduce_precision(mask_embed - high, 8, 7)
    low = mask_embed - high - middle
    mask_terms = jnp.stack([high, middle, low], axis=1).astype(BF16)
    embed = jnp.concatenate(
        [
            jnp.eye(channels, dtype=BF16),
            pad_columns(jnp.concatenate([bin_embed.T, mask_terms], axis=1)),
            pad_columns(col_embed.T),
            pad_columns(row_embed.T),
        ],
        axis=1,
    )
    gains = jnp.concatenate([layer_gain, final_gain[None]], axis=0)[:, :, None]
    w_in_t = jnp.swapaxes(w_in, 1, 2)
    w_out_t = jnp.swapaxes(w_out, 1, 2)
    weights = (
        jnp.concatenate([w_query.T, jnp.eye(pair_width, dtype=BF16)], axis=0),
        w_keyval.T,
        w_output.T,
        head_weight.T,
        head_weight,
        head_bias[:, None],
    )

    order = [group_count - 1] + list(range(1, group_count - 1)) + [0]
    sums = []
    for step in range(col_count):
        block = origin(col_me, col_count, step)
        features = []
        for turn in order:
            group = towards(tmpl_me, group_count, turn)
            offset = group * (residues // group_count) + row_offset + block * row_count
            place = jnp.stack([group, block, offset]).astype(jnp.int32)
            part = template_features(
                tmpl_act[0],
                tmpl_bins[0],
                place,
                masks,
                types,
                colmask,
                colhot,
                embed,
                gains,
                w_in_t,
                w_out_t,
                levels,
                row_count,
            )
            if turn:
                part = lax.ppermute(part, "tmpl", partners(group_count, turn))
            features.append(part)
        sums.append(pair_sums(features, pair_parts[step], label_parts[step], weights, residues))

    loss_part, head_part, output_part = [sum(parts[1:], parts[0]) for parts in zip(*sums)]
    bins = head_weight.shape[1]
    joined = jnp.concatenate(
        [head_part.reshape(-1), output_part.reshape(-1), jnp.sum(loss_part)[None]]
    )
    joined = lax.psum(joined, ("tmpl", "row", "col"))
    head_size = head_part.size
    head_all = joined[:head_size].reshape(head_part.shape)
    head_sum = head_all[:, :pair_width].T
    bias_sum = head_all[:, pair_width]
    output_sum = joined[head_size:-1].reshape(output_part.shape)
    loss_sum = joined[-1]
    squares = (
        jnp.sum(head_sum * head_sum)
        + jnp.sum(bias_sum * bias_sum)
        + jnp.sum(output_sum * output_sum)
    )
    factor = CLIP_NORM / jnp.maximum(jnp.sqrt(squares), CLIP_NORM)
    return (
        loss_sum / float(residues * residues),
        head_sum * factor,
        bias_sum * factor,
        output_sum * factor,
    )


def solution(mesh):
    in_specs = (
        P("tmpl", None, "row", None, "col"),
        P("tmpl", None, "row", "col"),
        P("tmpl", None),
        P("tmpl", None),
        P(("tmpl", "row", "col"), None, None),
        P(("tmpl", "row", "col"), None),
        P(),
        P(),
        P(),
        P(),
        P(),
        P(),
        P(),
        P(),
        P(),
        P(),
        P(),
        P(),
        P(),
    )
    out_specs = (P(), P(), P(), P())
    return jax.shard_map(
        on_device, mesh=mesh, in_specs=in_specs, out_specs=out_specs, check_vma=False
    )
```

time: 2660 us -> 1350 us (0.51)
  waiting for transfers between devices: 1490 us -> 684 us
  matrix products: 591 us -> 0 us
  Pallas kernels: 0 us -> 578 us
  other arithmetic: 352 us -> 9.93 us
  local copies, waits for them, and re-layouts: 158 us -> 34.9 us
  blocking collectives: 44.4 us -> 0 us
    all_to_all x1 -> x0, waiting for transfers between devices: 1490 us -> none  [on_device(): lax.all_to_all(features.reshape(1, group_count * col_count, row_count, ch...]
    dot_general x23 -> x0, matrix products: 591 us -> none  [the longest x8 329 us: embed_group(): jnp.einsum('nrej,ec->nrcj', hidden, w_out[layer_index], preferred_element...]
    pallas_call x0 -> x20, Pallas kernels: none -> 578 us  [the longest x16 353 us: template_features(): pl.pallas_call(functools.partial(template_kernel, levels, together), grid...]
    ppermute x0 -> x18, waiting for transfers between devices: none -> 562 us  [the longest x3 241 us: on_device(): pair = lax.ppermute(pair, 'col', partners(col_count, step))]
    reduce_sum x15 -> x1, other arithmetic: 202 us -> 0.61 us  [on_device(): jnp.sum(loss_part)[None]]
    psum x0 -> x1, waiting for transfers between devices: none -> 122 us  [on_device(): joined = lax.psum(joined, ('tmpl', 'row', 'col'))]
    slice x1 -> x2, local copies, waits for them, and re-layouts: 86.5 us -> 1.96 us  [the longest x1 1.19 us: on_device(): loss_sum = joined[-1]]
    unnamed x2 -> x0, other arithmetic: 54.6 us -> none
  transfers between devices with their start and end apart: 1 -> 19, of which waited for: 1 -> 7; matrix products, arithmetic and copies ran while one was open for 1% -> 2% of each run, Pallas kernels for 0% -> 37%
where the time goes in v1:
time: 1350 us
  waiting for transfers between devices  684 us (51%)
  Pallas kernels  578 us (43%)
  local copies, waits for them, and re-layouts  34.9 us (3%)
  starting transfers between devices  23.3 us (2%)
  between operations  18.2 us (1%)
    pallas_call x16, Pallas kernels, template_features(): pl.pallas_call(functools.partial(template_kernel, levels, together), grid...  353 us
    ppermute x3, waiting for transfers between devices, on_device(): pair = lax.ppermute(pair, 'col', partners(col_count, step))  241 us
    pallas_call x4, Pallas kernels, pair_sums(): pl.pallas_call(functools.partial(pair_kernel, together, residues), grid=(...  224 us
    ppermute x12, waiting for transfers between devices, on_device(): part = lax.ppermute(part, 'tmpl', partners(group_count, turn))  192 us
    ppermute x3, waiting for transfers between devices, on_device(): label = lax.ppermute(label, 'col', partners(col_count, step))  128 us
    psum x1, waiting for transfers between devices, on_device(): joined = lax.psum(joined, ('tmpl', 'row', 'col'))  122 us
  transfers between devices with their start and end apart: 19, of which 7 were waited for; matrix products, arithmetic and copies ran while one was open for 2% of the time, Pallas kernels for 37%

profile of v1, /device:TPU:10, one launch (start us, length us, event | category | flops | bytes accessed | tf_op | source)
XLA Modules:
  0.0 1348.4 jit_solution(2200474052240223600)
XLA Ops:
  17.1 22.0 %template_features.21 = bf16[64,64,512]{2,1,0:T(8,128)(2,1)} custom-call(s32[3]{0:T(128)S(1)} %pad_add_fusion.5.place_ref, s32[2048]{0:T(1024)S(1)} %bitcast.104, s32[2048]{0:T(1024)S(1)} %bitcast.120, bf16[4,256,64,512]{3,2,1,0:T(8,128)(2,1)} %bitcast.5.act_ref, s32[4,256,512]{2,1,0:T(8,128)S(1)} %bitcast.56, s32[1,512]{1,0:T(1,128)S(1)} %get-tuple-element.40.colmask_ref, ...), custom_call_target="tpu_custom_call" | custom-call | flops 7516192768 | bytes 8388608 | tf_op jit(solution)/shard_map/template_features/pallas_call | solution.py:126
  39.8 22.1 %template_features.22 = bf16[64,64,512]{2,1,0:T(8,128)(2,1)} custom-call(s32[3]{0:T(128)S(1)} %pad_add_fusion.6.place_ref, s32[2048]{0:T(1024)S(1)} %bitcast.105, s32[2048]{0:T(1024)S(1)} %bitcast.121, bf16[4,256,64,512]{3,2,1,0:T(8,128)(2,1)} %bitcast.5.act_ref, s32[4,256,512]{2,1,0:T(8,128)S(1)} %bitcast.57, s32[1,512]{1,0:T(1,128)S(1)} %get-tuple-element.40.colmask_ref, ...), custom_call_target="tpu_custom_call" | custom-call | flops 7516192768 | bytes 8388608 | tf_op jit(solution)/shard_map/template_features/pallas_call | solution.py:126
  90.7 22.0 %template_features.26 = bf16[64,64,512]{2,1,0:T(8,128)(2,1)} custom-call(s32[3]{0:T(128)S(1)} %pad_add_fusion.10.place_ref, s32[2048]{0:T(1024)S(1)} %bitcast.107, s32[2048]{0:T(1024)S(1)} %bitcast.123, bf16[4,256,64,512]{3,2,1,0:T(8,128)(2,1)} %bitcast.5.act_ref, s32[4,256,512]{2,1,0:T(8,128)S(1)} %bitcast.59, s32[1,512]{1,0:T(1,128)S(1)} %get-tuple-element.40.colmask_ref, ...), custom_call_target="tpu_custom_call" | custom-call | flops 7516192768 | bytes 8388608 | tf_op jit(solution)/shard_map/template_features/pallas_call | solution.py:126
  112.9 22.1 %template_features.25 = bf16[64,64,512]{2,1,0:T(8,128)(2,1)} custom-call(s32[3]{0:T(128)S(1)} %pad_add_fusion.9.place_ref, s32[2048]{0:T(1024)S(1)} %bitcast.108, s32[2048]{0:T(1024)S(1)} %bitcast.124, bf16[4,256,64,512]{3,2,1,0:T(8,128)(2,1)} %bitcast.5.act_ref, s32[4,256,512]{2,1,0:T(8,128)S(1)} %bitcast.60, s32[1,512]{1,0:T(1,128)S(1)} %get-tuple-element.40.colmask_ref, ...), custom_call_target="tpu_custom_call" | custom-call | flops 7516192768 | bytes 8388608 | tf_op jit(solution)/shard_map/template_features/pallas_call | solution.py:126
  135.0 22.0 %template_features.24 = bf16[64,64,512]{2,1,0:T(8,128)(2,1)} custom-call(s32[3]{0:T(128)S(1)} %pad_add_fusion.8.place_ref, s32[2048]{0:T(1024)S(1)} %bitcast.109, s32[2048]{0:T(1024)S(1)} %bitcast.125, bf16[4,256,64,512]{3,2,1,0:T(8,128)(2,1)} %bitcast.5.act_ref, s32[4,256,512]{2,1,0:T(8,128)S(1)} %bitcast.61, s32[1,512]{1,0:T(1,128)S(1)} %get-tuple-element.40.colmask_ref, ...), custom_call_target="tpu_custom_call" | custom-call | flops 7516192768 | bytes 8388608 | tf_op jit(solution)/shard_map/template_features/pallas_call | solution.py:126
  160.5 22.9 %constant_dynamic-slice_fusion.5 = (bf16[64,512,128]{2,1,0:T(8,128)(2,1)}, bf16[64,512,128]{2,1,0:T(8,128)(2,1)}, bf16[64,512,128]{2,1,0:T(8,128)(2,1)}, bf16[64,512,128]{2,1,0:T(8,128)(2,1)}) fusion(bf16[64,2048,128]{2,1,0:T(8,128)(2,1)} %param.23, s32[]{:T(128)S(6)} %select_n.9, s32[]{:T(128)S(6)} %select_n.8, s32[]{:T(128)S(6)} %select_n.21, s32[]{:T(128)S(6)} %select_n.20), kind=kLoop, calls=%fused_computation.37 | loop fusion | bytes 67108880 | tf_op jit(solution)/shard_map/dynamic_slice | solution.py:299
  183.5 62.1 %collective-permute-done.5.refs_2_ = bf16[64,64,512]{2,1,0:T(8,128)(2,1)} collective-permute-done((bf16[64,64,512]{2,1,0:T(8,128)(2,1)}, bf16[64,64,512]{2,1,0:T(8,128)(2,1)}, u32[]{:S(2)}, u32[]{:S(2)}) %collective-permute-start.5) | collective-permute-done | bytes 4194336 | tf_op jit(solution)/shard_map/ppermute | solution.py:367
  245.9 22.1 %template_features.17 = bf16[64,64,512]{2,1,0:T(8,128)(2,1)} custom-call(s32[3]{0:T(128)S(1)} %pad_add_fusion.1.place_ref, s32[2048]{0:T(1024)S(1)} %bitcast.110, s32[2048]{0:T(1024)S(1)} %bitcast.126, bf16[4,256,64,512]{3,2,1,0:T(8,128)(2,1)} %bitcast.5.act_ref, s32[4,256,512]{2,1,0:T(8,128)S(1)} %bitcast.62, s32[1,512]{1,0:T(1,128)S(1)} %get-tuple-element.40.colmask_ref, ...), custom_call_target="tpu_custom_call" | custom-call | flops 7516192768 | bytes 8388608 | tf_op jit(solution)/shard_map/template_features/pallas_call | solution.py:126
  292.1 22.0 %template_features.18 = bf16[64,64,512]{2,1,0:T(8,128)(2,1)} custom-call(s32[3]{0:T(128)S(1)} %pad_add_fusion.2.place_ref, s32[2048]{0:T(1024)S(1)} %bitcast.112, s32[2048]{0:T(1024)S(1)} %bitcast.128, bf16[4,256,64,512]{3,2,1,0:T(8,128)(2,1)} %bitcast.5.act_ref, s32[4,256,512]{2,1,0:T(8,128)S(1)} %bitcast.64, s32[1,512]{1,0:T(1,128)S(1)} %get-tuple-element.40.colmask_ref, ...), custom_call_target="tpu_custom_call" | custom-call | flops 7516192768 | bytes 8388608 | tf_op jit(solution)/shard_map/template_features/pallas_call | solution.py:126
  314.1 22.2 %template_features.16 = bf16[64,64,512]{2,1,0:T(8,128)(2,1)} custom-call(s32[3]{0:T(128)S(1)} %pad_add_fusion.place_ref, s32[2048]{0:T(1024)S(1)} %bitcast.113, s32[2048]{0:T(1024)S(1)} %bitcast.129, bf16[4,256,64,512]{3,2,1,0:T(8,128)(2,1)} %bitcast.5.act_ref, s32[4,256,512]{2,1,0:T(8,128)S(1)} %bitcast.65, s32[1,512]{1,0:T(1,128)S(1)} %get-tuple-element.40.colmask_ref, ...), custom_call_target="tpu_custom_call" | custom-call | flops 7516192768 | bytes 8388608 | tf_op jit(solution)/shard_map/template_features/pallas_call | solution.py:126
  336.4 87.5 %collective-permute-done.10.refs_2_ = bf16[64,64,512]{2,1,0:T(8,128)(2,1)} collective-permute-done((bf16[64,64,512]{2,1,0:T(8,128)(2,1)}, bf16[64,64,512]{2,1,0:T(8,128)(2,1)}, u32[]{:S(2)}, u32[]{:S(2)}) %collective-permute-start.10) | collective-permute-done | bytes 4194336 | tf_op jit(solution)/shard_map/ppermute | solution.py:367
  429.6 22.1 %template_features.27.refs_3_ = bf16[64,64,512]{2,1,0:T(8,128)(2,1)} custom-call(s32[3]{0:T(128)S(1)} %pad_add_fusion.11.place_ref, s32[2048]{0:T(1024)S(1)} %bitcast.114, s32[2048]{0:T(1024)S(1)} %bitcast.130, bf16[4,256,64,512]{3,2,1,0:T(8,128)(2,1)} %bitcast.5.act_ref, s32[4,256,512]{2,1,0:T(8,128)S(1)} %bitcast.66, ...), custom_call_target="tpu_custom_call" | custom-call | flops 7516192768 | bytes 8388608 | tf_op jit(solution)/shard_map/template_features/pallas_call | solution.py:126
  495.1 22.0 %template_features.30 = bf16[64,64,512]{2,1,0:T(8,128)(2,1)} custom-call(s32[3]{0:T(128)S(1)} %pad_add_fusion.14.place_ref, s32[2048]{0:T(1024)S(1)} %bitcast.116, s32[2048]{0:T(1024)S(1)} %bitcast.132, bf16[4,256,64,512]{3,2,1,0:T(8,128)(2,1)} %bitcast.5.act_ref, s32[4,256,512]{2,1,0:T(8,128)S(1)} %bitcast.68, s32[1,512]{1,0:T(1,128)S(1)} %get-tuple-element.40.colmask_ref, ...), custom_call_target="tpu_custom_call" | custom-call | flops 7516192768 | bytes 8388608 | tf_op jit(solution)/shard_map/template_features/pallas_call | solution.py:126
  517.1 22.0 %template_features.28 = bf16[64,64,512]{2,1,0:T(8,128)(2,1)} custom-call(s32[3]{0:T(128)S(1)} %pad_add_fusion.12.place_ref, s32[2048]{0:T(1024)S(1)} %bitcast.117, s32[2048]{0:T(1024)S(1)} %bitcast.133, bf16[4,256,64,512]{3,2,1,0:T(8,128)(2,1)} %bitcast.5.act_ref, s32[4,256,512]{2,1,0:T(8,128)S(1)} %bitcast.69, s32[1,512]{1,0:T(1,128)S(1)} %get-tuple-element.40.colmask_ref, ...), custom_call_target="tpu_custom_call" | custom-call | flops 7516192768 | bytes 8388608 | tf_op jit(solution)/shard_map/template_features/pallas_call | solution.py:126
  539.2 22.1 %template_features.31.refs_3_ = bf16[64,64,512]{2,1,0:T(8,128)(2,1)} custom-call(s32[3]{0:T(128)S(1)} %pad_add_fusion.15.place_ref, s32[2048]{0:T(1024)S(1)} %bitcast.118, s32[2048]{0:T(1024)S(1)} %bitcast.134, bf16[4,256,64,512]{3,2,1,0:T(8,128)(2,1)} %bitcast.5.act_ref, s32[4,256,512]{2,1,0:T(8,128)S(1)} %bitcast.70, ...), custom_call_target="tpu_custom_call" | custom-call | flops 7516192768 | bytes 8388608 | tf_op jit(solution)/shard_map/template_features/pallas_call | solution.py:126
  561.2 22.4 %template_features.19.refs_3_ = bf16[64,64,512]{2,1,0:T(8,128)(2,1)} custom-call(s32[3]{0:T(128)S(1)} %pad_add_fusion.3.place_ref, s32[2048]{0:T(1024)S(1)} %bitcast.119, s32[2048]{0:T(1024)S(1)} %bitcast.135, bf16[4,256,64,512]{3,2,1,0:T(8,128)(2,1)} %bitcast.5.act_ref, s32[4,256,512]{2,1,0:T(8,128)S(1)} %bitcast.71, ...), custom_call_target="tpu_custom_call" | custom-call | flops 7516192768 | bytes 8388608 | tf_op jit(solution)/shard_map/template_features/pallas_call | solution.py:126
  583.7 24.0 %collective-permute-done.2.refs_2_ = bf16[64,64,512]{2,1,0:T(8,128)(2,1)} collective-permute-done((bf16[64,64,512]{2,1,0:T(8,128)(2,1)}, bf16[64,64,512]{2,1,0:T(8,128)(2,1)}, u32[]{:S(2)}, u32[]{:S(2)}) %collective-permute-start.2) | collective-permute-done | bytes 4194336 | tf_op jit(solution)/shard_map/ppermute | solution.py:367
  611.2 56.1 %pair_sums.4 = (f32[1,512]{1,0:T(1,128)S(1)}, f32[64,144]{1,0:T(8,128)S(1)}, f32[64,128]{1,0:T(8,128)S(1)}) custom-call(bf16[64,64,512]{2,1,0:T(8,128)(2,1)} %collective-permute-done.refs_0_, bf16[64,64,512]{2,1,0:T(8,128)(2,1)} %copy-done.20, bf16[64,64,512]{2,1,0:T(8,128)(2,1)} %collective-permute-done.2.refs_2_, ...), custom_call_target="tpu_custom_call" | custom-call | flops 19327352832 | bytes 25165824 | tf_op jit(solution)/shard_map/pair_sums/pallas_call | solution.py:227
  667.4 56.2 %pair_sums.5 = (f32[1,512]{1,0:T(1,128)S(1)}, f32[64,144]{1,0:T(8,128)S(1)}, f32[64,128]{1,0:T(8,128)S(1)}) custom-call(bf16[64,64,512]{2,1,0:T(8,128)(2,1)} %collective-permute-done.3.refs_0_, bf16[64,64,512]{2,1,0:T(8,128)(2,1)} %collective-permute-done.4.refs_1_, bf16[64,64,512]{2,1,0:T(8,128)(2,1)} %collective-permute-done.5.refs_2_, ...), custom_call_target="tpu_custom_call" | custom-call | flops 19327352832 | bytes 25165824 | tf_op jit(solution)/shard_map/pair_sums/pallas_call | solution.py:227
  723.6 241.2 %collective-permute-done.11.refs_4_ = bf16[64,512,128]{2,1,0:T(8,128)(2,1)} collective-permute-done((bf16[64,512,128]{2,1,0:T(8,128)(2,1)}, bf16[64,512,128]{2,1,0:T(8,128)(2,1)}, u32[]{:S(2)}, u32[]{:S(2)}) %collective-permute-start.11) | collective-permute-done | bytes 8388640 | tf_op jit(solution)/shard_map/ppermute | solution.py:306
  965.4 56.1 %pair_sums.6 = (f32[1,512]{1,0:T(1,128)S(1)}, f32[64,144]{1,0:T(8,128)S(1)}, f32[64,128]{1,0:T(8,128)S(1)}) custom-call(bf16[64,64,512]{2,1,0:T(8,128)(2,1)} %collective-permute-done.8.refs_0_, bf16[64,64,512]{2,1,0:T(8,128)(2,1)} %collective-permute-done.9.refs_1_, bf16[64,64,512]{2,1,0:T(8,128)(2,1)} %collective-permute-done.10.refs_2_, ...), custom_call_target="tpu_custom_call" | custom-call | flops 19327352832 | bytes 25165824 | tf_op jit(solution)/shard_map/pair_sums/pallas_call | solution.py:227
  1021.6 128.4 %collective-permute-done.17.refs_5_ = s32[64,512]{1,0:T(8,128)S(1)} collective-permute-done((s32[64,512]{1,0:T(8,128)S(1)}, s32[64,512]{1,0:T(8,128)S(1)}, u32[]{:S(2)}, u32[]{:S(2)}) %collective-permute-start.17) | collective-permute-done | bytes 131104 | tf_op jit(solution)/shard_map/ppermute | solution.py:307
  1150.0 56.0 %pair_sums.7 = (f32[1,512]{1,0:T(1,128)S(1)}, f32[64,144]{1,0:T(8,128)S(1)}, f32[64,128]{1,0:T(8,128)S(1)}) custom-call(bf16[64,64,512]{2,1,0:T(8,128)(2,1)S(1)} %collective-permute-done.13.refs_0_, bf16[64,64,512]{2,1,0:T(8,128)(2,1)} %collective-permute-done.14.refs_1_, bf16[64,64,512]{2,1,0:T(8,128)(2,1)} %collective-permute-done.15.refs_2_, ...), custom_call_target="tpu_custom_call" | custom-call | flops 19327352832 | bytes 25165824 | tf_op jit(solution)/shard_map/pair_sums/pallas_call | solution.py:227
  1208.0 122.4 %all-reduce.5.cloned.1.call-done = f32[17409]{0:T(1024)} async-done(((f32[17409]{0:T(1024)}), f32[17409]{0:T(1024)}) %all-reduce.5.cloned.1.call-update) | async-done | bytes 69652 | tf_op jit(solution)/shard_map/psum | solution.py:376
  (130 shorter events, 130.0 us)
Async XLA Ops:
  7.2 1323.3 %all-reduce.5.cloned.1.call-start = ((), (), s32[]{:S(2)}) async-start(), calls=%async_computation | async-start | bytes 147456 | tf_op jit(solution)/shard_map/psum | solution.py:376
  39.2 119.9 %collective-permute-start.4 = (bf16[64,64,512]{2,1,0:T(8,128)(2,1)}, bf16[64,64,512]{2,1,0:T(8,128)(2,1)}, u32[]{:S(2)}, u32[]{:S(2)}) collective-permute-start(bf16[64,64,512]{2,1,0:T(8,128)(2,1)} %template_features.21), channel_id=1, source_target_pairs={{0,8},{8,0},{16,24},{24,16},{1,9},{9,1},{17,25},{25,17},{2,10},{10... | collective-permute-start | bytes 12582920 | tf_op jit(solution)/shard_map/ppermute | solution.py:367
  61.8 183.7 %collective-permute-start.5 = (bf16[64,64,512]{2,1,0:T(8,128)(2,1)}, bf16[64,64,512]{2,1,0:T(8,128)(2,1)}, u32[]{:S(2)}, u32[]{:S(2)}) collective-permute-start(bf16[64,64,512]{2,1,0:T(8,128)(2,1)} %template_features.22), channel_id=1, source_target_pairs={{0,16},{8,24},{16,0},{24,8},{1,17},{9,25},{17,1},{25,9},{2,18},{10... | collective-permute-start | bytes 12582920 | tf_op jit(solution)/shard_map/ppermute | solution.py:367
  85.5 182.5 %collective-permute-start.3 = (bf16[64,64,512]{2,1,0:T(8,128)(2,1)}, bf16[64,64,512]{2,1,0:T(8,128)(2,1)}, u32[]{:S(2)}, u32[]{:S(2)}) collective-permute-start(bf16[64,64,512]{2,1,0:T(8,128)(2,1)} %template_features.20), channel_id=1, source_target_pairs={{0,24},{8,16},{16,8},{24,0},{1,25},{9,17},{17,9},{25,1},{2,26},{10... | collective-permute-start | bytes 12582920 | tf_op jit(solution)/shard_map/ppermute | solution.py:367
  87.6 69.4 %collective-permute-start.7 = (s32[64,512]{1,0:T(8,128)S(1)}, s32[64,512]{1,0:T(8,128)S(1)}, u32[]{:S(2)}, u32[]{:S(2)}) collective-permute-start(s32[64,512]{1,0:T(8,128)S(1)} %get-tuple-element.32), channel_id=1, source_target_pairs={{0,1},{1,0},{2,3},{3,2},{4,5},{5,4},{6,7},{7,6},{8,9},{9,8},{10,11... | collective-permute-start | bytes 393224 | tf_op jit(solution)/shard_map/ppermute | solution.py:307
  88.1 70.5 %collective-permute-start.12 = (s32[64,512]{1,0:T(8,128)S(1)}, s32[64,512]{1,0:T(8,128)S(1)}, u32[]{:S(2)}, u32[]{:S(2)}) collective-permute-start(s32[64,512]{1,0:T(8,128)S(1)} %get-tuple-element.35), channel_id=1, source_target_pairs={{0,2},{1,3},{2,0},{3,1},{4,6},{5,7},{6,4},{7,5},{8,10},{9,11},{10,... | collective-permute-start | bytes 393224 | tf_op jit(solution)/shard_map/ppermute | solution.py:307
  157.0 266.8 %collective-permute-start.10 = (bf16[64,64,512]{2,1,0:T(8,128)(2,1)}, bf16[64,64,512]{2,1,0:T(8,128)(2,1)}, u32[]{:S(2)}, u32[]{:S(2)}) collective-permute-start(bf16[64,64,512]{2,1,0:T(8,128)(2,1)} %template_features.26), channel_id=1, source_target_pairs={{0,16},{8,24},{16,0},{24,8},{1,17},{9,25},{17,1},{25,9},{2,18},{10... | collective-permute-start | bytes 12582920 | tf_op jit(solution)/shard_map/ppermute | solution.py:367
  158.5 268.1 %collective-permute-start.9 = (bf16[64,64,512]{2,1,0:T(8,128)(2,1)}, bf16[64,64,512]{2,1,0:T(8,128)(2,1)}, u32[]{:S(2)}, u32[]{:S(2)}) collective-permute-start(bf16[64,64,512]{2,1,0:T(8,128)(2,1)} %template_features.25), channel_id=1, source_target_pairs={{0,8},{8,0},{16,24},{24,16},{1,9},{9,1},{17,25},{25,17},{2,10},{10... | collective-permute-start | bytes 12582920 | tf_op jit(solution)/shard_map/ppermute | solution.py:367
  159.1 269.1 %collective-permute-start.8 = (bf16[64,64,512]{2,1,0:T(8,128)(2,1)}, bf16[64,64,512]{2,1,0:T(8,128)(2,1)}, u32[]{:S(2)}, u32[]{:S(2)}) collective-permute-start(bf16[64,64,512]{2,1,0:T(8,128)(2,1)} %template_features.24), channel_id=1, source_target_pairs={{0,24},{8,16},{16,8},{24,0},{1,25},{9,17},{17,9},{25,1},{2,26},{10... | collective-permute-start | bytes 12582920 | tf_op jit(solution)/shard_map/ppermute | solution.py:367
  245.5 365.2 %collective-permute-start.6 = (bf16[64,512,128]{2,1,0:T(8,128)(2,1)}, bf16[64,512,128]{2,1,0:T(8,128)(2,1)}, u32[]{:S(2)}, u32[]{:S(2)}) collective-permute-start(bf16[64,512,128]{2,1,0:T(8,128)(2,1)} %get-tuple-element.28), channel_id=1, source_target_pairs={{0,1},{1,0},{2,3},{3,2},{4,5},{5,4},{6,7},{7,6},{8,9},{9,8},{10,11... | collective-permute-start | bytes 25165832 | tf_op jit(solution)/shard_map/ppermute | solution.py:306
  267.9 224.5 %collective-permute-start.1 = (bf16[64,64,512]{2,1,0:T(8,128)(2,1)}, bf16[64,64,512]{2,1,0:T(8,128)(2,1)S(1)}, u32[]{:S(2)}, u32[]{:S(2)}) collective-permute-start(bf16[64,64,512]{2,1,0:T(8,128)(2,1)} %template_features.17), channel_id=1, source_target_pairs={{0,8},{8,0},{16,24},{24,16},{1,9},{9,1},{17,25},{25,17},{2,10},{10... | collective-permute-start | bytes 12582920 | tf_op jit(solution)/shard_map/ppermute | solution.py:367
  423.8 541.0 %collective-permute-start.11 = (bf16[64,512,128]{2,1,0:T(8,128)(2,1)}, bf16[64,512,128]{2,1,0:T(8,128)(2,1)}, u32[]{:S(2)}, u32[]{:S(2)}) collective-permute-start(bf16[64,512,128]{2,1,0:T(8,128)(2,1)} %get-tuple-element.31), channel_id=1, source_target_pairs={{0,2},{1,3},{2,0},{3,1},{4,6},{5,7},{6,4},{7,5},{8,10},{9,11},{10,... | collective-permute-start | bytes 25165832 | tf_op jit(solution)/shard_map/ppermute | solution.py:306
  426.6 181.1 %collective-permute-start.2 = (bf16[64,64,512]{2,1,0:T(8,128)(2,1)}, bf16[64,64,512]{2,1,0:T(8,128)(2,1)}, u32[]{:S(2)}, u32[]{:S(2)}) collective-permute-start(bf16[64,64,512]{2,1,0:T(8,128)(2,1)} %template_features.18), channel_id=1, source_target_pairs={{0,16},{8,24},{16,0},{24,8},{1,17},{9,25},{17,1},{25,9},{2,18},{10... | collective-permute-start | bytes 12582920 | tf_op jit(solution)/shard_map/ppermute | solution.py:367
  428.2 181.0 %collective-permute-start = (bf16[64,64,512]{2,1,0:T(8,128)(2,1)}, bf16[64,64,512]{2,1,0:T(8,128)(2,1)}, u32[]{:S(2)}, u32[]{:S(2)}) collective-permute-start(bf16[64,64,512]{2,1,0:T(8,128)(2,1)} %template_features.16), channel_id=1, source_target_pairs={{0,24},{8,16},{16,8},{24,0},{1,25},{9,17},{17,9},{25,1},{2,26},{10... | collective-permute-start | bytes 12582920 | tf_op jit(solution)/shard_map/ppermute | solution.py:367
  451.7 43.4 %copy-start.18 = (bf16[128,64]{0,1:T(8,128)(2,1)S(1)}, bf16[128,64]{0,1:T(8,128)(2,1)}, u32[]{:S(2)}) copy-start(bf16[128,64]{0,1:T(8,128)(2,1)} %param.33) | copy-start | bytes 49156
  492.5 657.5 %collective-permute-start.16 = (bf16[64,512,128]{2,1,0:T(8,128)(2,1)}, bf16[64,512,128]{2,1,0:T(8,128)(2,1)}, u32[]{:S(2)}, u32[]{:S(2)}) collective-permute-start(bf16[64,512,128]{2,1,0:T(8,128)(2,1)} %get-tuple-element.30), channel_id=1, source_target_pairs={{0,3},{1,2},{2,1},{3,0},{4,7},{5,6},{6,5},{7,4},{8,11},{9,10},{10,... | collective-permute-start | bytes 25165832 | tf_op jit(solution)/shard_map/ppermute | solution.py:306
  561.2 46.5 %copy-start.13 = (bf16[64,64,512]{2,1,0:T(8,128)(2,1)S(1)}, bf16[64,64,512]{2,1,0:T(8,128)(2,1)}, u32[]{:S(2)}) copy-start(bf16[64,64,512]{2,1,0:T(8,128)(2,1)} %template_features.29) | copy-start | bytes 12582916
  607.7 542.2 %collective-permute-start.14 = (bf16[64,64,512]{2,1,0:T(8,128)(2,1)S(1)}, bf16[64,64,512]{2,1,0:T(8,128)(2,1)}, u32[]{:S(2)}, u32[]{:S(2)}) collective-permute-start(bf16[64,64,512]{2,1,0:T(8,128)(2,1)S(1)} %copy-done.13), channel_id=1, source_target_pairs={{0,8},{8,0},{16,24},{24,16},{1,9},{9,1},{17,25},{25,17},{2,10},{10... | collective-permute-start | bytes 12582920 | tf_op jit(solution)/shard_map/ppermute | solution.py:367
  609.2 540.8 %collective-permute-start.15 = (bf16[64,64,512]{2,1,0:T(8,128)(2,1)}, bf16[64,64,512]{2,1,0:T(8,128)(2,1)}, u32[]{:S(2)}, u32[]{:S(2)}) collective-permute-start(bf16[64,64,512]{2,1,0:T(8,128)(2,1)} %template_features.30), channel_id=1, source_target_pairs={{0,16},{8,24},{16,0},{24,8},{1,17},{9,25},{17,1},{25,9},{2,18},{10... | collective-permute-start | bytes 12582920 | tf_op jit(solution)/shard_map/ppermute | solution.py:367
  610.7 539.3 %collective-permute-start.13 = (bf16[64,64,512]{2,1,0:T(8,128)(2,1)}, bf16[64,64,512]{2,1,0:T(8,128)(2,1)S(1)}, u32[]{:S(2)}, u32[]{:S(2)}) collective-permute-start(bf16[64,64,512]{2,1,0:T(8,128)(2,1)} %template_features.28), channel_id=1, source_target_pairs={{0,24},{8,16},{16,8},{24,0},{1,25},{9,17},{17,9},{25,1},{2,26},{10... | collective-permute-start | bytes 12582920 | tf_op jit(solution)/shard_map/ppermute | solution.py:367
  611.2 56.1 %copy-start.12 = (s32[64,512]{1,0:T(8,128)S(1)}, s32[64,512]{1,0:T(8,128)}, u32[]{:S(2)}) copy-start(s32[64,512]{1,0:T(8,128)} %copy-done.11) | copy-start | bytes 393220
  667.4 297.4 %copy-start.15 = (s32[64,512]{1,0:T(8,128)S(1)}, s32[64,512]{1,0:T(8,128)}, u32[]{:S(2)}) copy-start(s32[64,512]{1,0:T(8,128)} %get-tuple-element.34) | copy-start | bytes 393220
  667.4 298.0 %copy-start.10 = (s32[64,512]{1,0:T(8,128)S(1)}, s32[64,512]{1,0:T(8,128)}, u32[]{:S(2)}) copy-start(s32[64,512]{1,0:T(8,128)} %copy-done.9) | copy-start | bytes 393220
  964.8 185.2 %collective-permute-start.17 = (s32[64,512]{1,0:T(8,128)S(1)}, s32[64,512]{1,0:T(8,128)S(1)}, u32[]{:S(2)}, u32[]{:S(2)}) collective-permute-start(s32[64,512]{1,0:T(8,128)S(1)} %copy-done.15), channel_id=1, source_target_pairs={{0,3},{1,2},{2,1},{3,0},{4,7},{5,6},{6,5},{7,4},{8,11},{9,10},{10,... | collective-permute-start | bytes 393224 | tf_op jit(solution)/shard_map/ppermute | solution.py:307
  (16 other events, 343.6 us)
Sparse Core Ops, SparseCore 0:
  1208.2 122.2 all-reduce.4
